TPU v7x, 512 devices: a whole 4x8x8 slice. The times are simulated.
512 devices in a mesh: side: 8 (over y_lo, x), ep: 8 (over y_hi, core), tp: 8 (over z).
Axes of the slice: x: 4, y: 8 (y_hi: 4, y_lo: 2; y = y_hi * 2 + y_lo), z: 8, core: 2. Of those that a mesh axis runs over, the one named last changes fastest.
Arguments:
- rows: bfloat16 [512, 6144], P(('ep', 'tp'), 'side'), may hold values from -6 to 6
- expert_ids: int32 [512, 2], P(('ep', 'tp')), may hold values from 0 to 7, all different within a row; in each aligned block of 8 rows (0 to 7, 8 to 15, ...) at most 4 rows name the same one
- combine: float32 [512, 2], P(('ep', 'tp')), may hold values from 0.2 to 1
- w_gate: bfloat16 [8, 6144, 8192], P('ep', 'side', 'tp'), may hold values from -0.078125 to 0.078125
- w_up: bfloat16 [8, 6144, 8192], P('ep', 'side', 'tp'), may hold values from -0.078125 to 0.078125
- w_down: bfloat16 [8, 8192, 6144], P('ep', 'tp', 'side'), may hold values from -0.0625 to 0.0625
Outputs:
- mixed: bfloat16 [512, 6144], P(('ep', 'tp'), 'side')
Inputs may be any that keep to these rules, and one draw needn't show every extreme that they name: `expert_ids`: each row names 2 different experts; within the 8 rows of one device no expert is named by more than 4 rows, a bound that some block reaches.
All inputs are finite; a program needn't handle non-finite values.
Results may differ from a plain program's by a relative error of at most 0.034.
Values may be sent and summed in bfloat16 or wider, within the bound.
No kernel may reach another device: no remote copies, remote signals or barrier semaphores. Data moves between devices by JAX's collectives and lax.ppermute only.
A program may use at most 64 MiB of HBM per device.

v0:
```python
import jax
import jax.numpy as jnp
from jax import lax
from jax.sharding import PartitionSpec as P

TOP = 2


def local(rows, expert_ids, combine, w_gate, w_up, w_down):
    tok_rows, width = rows.shape
    ep_count = lax.axis_size("ep")
    tp_count = lax.axis_size("tp")
    capacity = max(2, tok_rows // 2, tok_rows * TOP // ep_count)
    chosen = expert_ids[:, :, None] == jnp.arange(ep_count, dtype=jnp.int32)[None, None, :]
    member = jnp.any(chosen, axis=1)
    ranking = jnp.cumsum(member.astype(jnp.int32), axis=0) - 1
    places = jnp.arange(capacity, dtype=jnp.int32)
    placing = member[None, :, :] & (ranking[None, :, :] == places[:, None, None])
    placing = jnp.transpose(placing, (2, 0, 1)).astype(jnp.bfloat16)
    outgoing = jnp.einsum("ect,td->ecd", placing, rows, preferred_element_type=jnp.float32).astype(
        jnp.bfloat16
    )
    spread = jnp.broadcast_to(outgoing[:, None], (ep_count, tp_count, capacity, width))
    spread = spread.reshape(ep_count * tp_count, capacity, width)
    arrived = lax.all_to_all(spread, ("ep", "tp"), split_axis=0, concat_axis=0, tiled=True)
    arrived = arrived.reshape(ep_count, tp_count, capacity, width).transpose(1, 0, 2, 3)
    slots = arrived.reshape(-1, width)
    gate_part = jnp.dot(slots, w_gate[0], preferred_element_type=jnp.float32)
    up_part = jnp.dot(slots, w_up[0], preferred_element_type=jnp.float32)
    gate, up = (
        lax.psum(gate_part.astype(jnp.bfloat16), "side").astype(jnp.float32),
        lax.psum(up_part.astype(jnp.bfloat16), "side").astype(jnp.float32),
    )
    hidden = (jax.nn.silu(gate) * up).astype(jnp.bfloat16)
    down_local = w_down[0]
    own_rows = ep_count * capacity
    summed = lax.psum(
        jnp.dot(hidden, down_local, preferred_element_type=jnp.float32).astype(jnp.bfloat16), "tp"
    ).astype(jnp.float32)
    mine = lax.dynamic_slice_in_dim(summed, lax.axis_index("tp") * own_rows, own_rows, 0)
    expert_out = mine.astype(jnp.bfloat16).reshape(ep_count, capacity, width)
    returned = lax.all_to_all(expert_out, "ep", split_axis=0, concat_axis=0, tiled=True)
    gathered = jnp.einsum("ect,ecd->etd", placing, returned, preferred_element_type=jnp.float32)
    weighting = jnp.einsum("tk,tke->et", combine, chosen.astype(jnp.float32))
    mixed = jnp.sum(weighting[:, :, None] * gathered, axis=0)
    return mixed.astype(jnp.bfloat16)


def solution(mesh):
    return jax.shard_map(
        local,
        mesh=mesh,
        in_specs=(
            P(("ep", "tp"), "side"),
            P(("ep", "tp"), None),
            P(("ep", "tp"), None),
            P("ep", "side", "tp"),
            P("ep", "side", "tp"),
            P("ep", "tp", "side"),
        ),
        out_specs=P(("ep", "tp"), "side"),
        check_vma=False,
    )
```

profile of v0, /device:TPU:1, one launch (start us, length us, event | category | flops | bytes accessed | tf_op | source)
XLA Modules:
  0.0 236.8 jit_solution(13446510896408773316)
XLA Ops:
  6.5 0.0 copy-start
  6.5 0.0 all-reduce.6.cloned.1.call-start
  6.5 0.9 fusion.26
  7.5 0.1 copy.22
  7.5 0.1 copy.21
  7.6 0.8 convolution_convert_fusion
  8.5 0.1 broadcast_in_dim.2
  8.6 33.9 %all_to_all.10 = bf16[64,4,768]{2,1,0:T(4,128)(2,1)S(1)} all-to-all(bf16[64,4,768]{2,1,0:T(4,128)(2,1)S(1)} %bitcast.32), channel_id=1, replica_groups=mesh['side'=8,'ep'=8,'tp'=8] {'ep','tp'}, dimensions={0} | all-to-all | bytes 786432 | tf_op jit(solution)/shard_map/all_to_all | solution.py:25
  42.6 1.0 copy.26
  43.6 0.0 copy-start.1
  43.6 1.2 reshape.27
  44.9 0.0 copy-done
  44.9 1.4 fusion.6
  46.3 0.0 copy-done.1
  46.3 1.4 fusion.9
  47.7 0.0 all-reduce.6.cloned.1.call-update
  47.7 0.0 all-reduce.4.cloned.1.call-start
  47.7 78.2 %all-reduce.6.cloned.1.call-done = (bf16[256,1024]{1,0:T(8,128)(2,1)}, bf16[256,1024]{1,0:T(8,128)(2,1)}) async-done(((bf16[256,1024]{1,0:T(8,128)(2,1)}, bf16[256,1024]{1,0:T(8,128)(2,1)}), (bf16[256,1024]{1,0:T(8,128)(2,1)}, bf16[256,1024]{1,0:T(8,128)(2,1)})) %all-reduce.6.cloned.1.call-update) | async-done | bytes 1048592 | tf_op jit(solution)/shard_map/psum | solution.py:32
  125.9 0.0 copy-start.2
  125.9 0.0 copy-start.3
  125.9 3.3 %fusion.12 = bf16[256,768]{1,0:T(8,128)(2,1)} fusion(bf16[1,1024,768]{2,1,0:T(8,128)(2,1)} %param.11, bf16[256,1024]{1,0:T(8,128)(2,1)} %get-tuple-element.5, bf16[256,1024]{1,0:T(8,128)(2,1)} %get-tuple-element.6), kind=kOutput, calls=%fused_computation.10 | convolution fusion | flops 404946944 | bytes 3014656 | tf_op jit(solution)/shard_map/dot_general | solution.py:38
  129.1 0.0 all-reduce.4.cloned.1.call-update
  129.2 79.4 %all-reduce.4.cloned.1.call-done = bf16[256,768]{1,0:T(8,128)(2,1)} async-done(((bf16[256,768]{1,0:T(8,128)(2,1)}), bf16[256,768]{1,0:T(8,128)(2,1)}) %all-reduce.4.cloned.1.call-update) | async-done | bytes 393232 | tf_op jit(solution)/shard_map/psum | solution.py:37
  208.6 0.8 convert_convert_fusion
  209.4 0.6 reshape.28
  210.0 11.8 %all-to-all-start.1 = ((bf16[8,4,768]{2,1,0:T(4,128)(2,1)}), bf16[8,4,768]{2,1,0:T(4,128)(2,1)S(1)}, u32[]{:S(2)}, u32[]{:S(2)}) async-start(bf16[8,4,768]{2,1,0:T(4,128)(2,1)} %reshape.28), calls=%async_computation.1 | async-start | bytes 98304 | tf_op jit(solution)/shard_map/all_to_all | solution.py:42
  221.8 0.0 copy-done.2
  221.8 0.0 copy-done.3
  221.8 0.1 select_reduce_fusion
  221.9 0.1 copy.31
  222.0 7.2 %all-to-all-done.1 = bf16[8,4,768]{2,1,0:T(4,128)(2,1)S(1)} async-done(((bf16[8,4,768]{2,1,0:T(4,128)(2,1)}), bf16[8,4,768]{2,1,0:T(4,128)(2,1)S(1)}, u32[]{:S(2)}, u32[]{:S(2)}) %all-to-all-start.1) | async-done | bytes 49184 | tf_op jit(solution)/shard_map/all_to_all | solution.py:42
  229.1 0.8 fusion.15
  (6 shorter events, 0.1 us)
Async XLA Ops:
  6.5 38.3 %copy-start = (bf16[1,768,1024]{2,1,0:T(8,128)(2,1)S(1)}, bf16[1,768,1024]{2,1,0:T(8,128)(2,1)}, u32[]{:S(2)}) copy-start(bf16[1,768,1024]{2,1,0:T(8,128)(2,1)} %param.9) | copy-start | bytes 4718596
  6.5 119.3 %all-reduce.6.cloned.1.call-start = ((), (), s32[]{:S(2)}) async-start(), calls=%async_computation.3 | async-start | bytes 2097152 | tf_op jit(solution)/shard_map/psum | solution.py:32
  43.6 2.6 %copy-start.1 = (bf16[1,768,1024]{2,1,0:T(8,128)(2,1)S(1)}, bf16[1,768,1024]{2,1,0:T(8,128)(2,1)}, u32[]{:S(2)}) copy-start(bf16[1,768,1024]{2,1,0:T(8,128)(2,1)} %param.10) | copy-start | bytes 4718596
  47.7 160.9 %all-reduce.4.cloned.1.call-start = ((), (), s32[]{:S(2)}) async-start(), calls=%async_computation.2 | async-start | bytes 786432 | tf_op jit(solution)/shard_map/psum | solution.py:37
  125.9 95.9 %copy-start.2 = (s32[8,2]{0,1:T(2,128)S(1)}, s32[8,2]{0,1:T(2,128)}, u32[]{:S(2)}) copy-start(s32[8,2]{0,1:T(2,128)} %param.7) | copy-start | bytes 196
  125.9 95.9 %copy-start.3 = (f32[8,2]{0,1:T(2,128)S(1)}, f32[8,2]{0,1:T(2,128)}, u32[]{:S(2)}) copy-start(f32[8,2]{0,1:T(2,128)} %param.8) | copy-start | bytes 196
  210.0 19.1 %all-to-all-start.1 = ((bf16[8,4,768]{2,1,0:T(4,128)(2,1)}), bf16[8,4,768]{2,1,0:T(4,128)(2,1)S(1)}, u32[]{:S(2)}, u32[]{:S(2)}) async-start(bf16[8,4,768]{2,1,0:T(4,128)(2,1)} %reshape.28), calls=%async_computation.1 | async-start | bytes 98304 | tf_op jit(solution)/shard_map/all_to_all | solution.py:42
Sparse Core Ops, SparseCore 0:
  47.8 78.0 all-reduce.5
  129.3 79.2 all-reduce.3
where the time goes:
time: 237 us
  waiting for transfers between devices  165 us (70%)
  blocking collectives  33.9 us (14%)
  between operations  13.5 us (6%)
  starting transfers between devices  11.8 us (5%)
  matrix products  7.7 us (3%)
  local copies, waits for them, and re-layouts  3.3 us (1%)
    psum x1, waiting for transfers between devices, local(): lax.psum(jnp.dot(hidden, down_local, preferred_element_type=jnp.float32)....  79.4 us
    psum x1, waiting for transfers between devices, local(): lax.psum(up_part.astype(jnp.bfloat16), 'side').astype(jnp.float32)  78.2 us
    all_to_all x1, blocking collectives, local(): lax.all_to_all(spread, ('ep', 'tp'), split_axis=0, concat_axis=0, tiled=T...  33.9 us
    all_to_all x1, starting transfers between devices, local(): lax.all_to_all(expert_out, 'ep', split_axis=0, concat_axis=0, tiled=True)  11.8 us
    all_to_all x1, waiting for transfers between devices, local(): lax.all_to_all(expert_out, 'ep', split_axis=0, concat_axis=0, tiled=True)  7.16 us
  transfers between devices with their start and end apart: 3, of which 3 were waited for; matrix products, arithmetic and copies ran while one was open for 0% of the time, Pallas kernels for 0%

commit v1 on v0

v1 whole, which is shorter than its diff:
```python
import functools

import jax
import jax.numpy as jnp
from jax import lax
from jax.experimental import pallas as pl
from jax.experimental.pallas import tpu as pltpu
from jax.sharding import Mesh
from jax.sharding import PartitionSpec as P

BF, F32 = jnp.bfloat16, jnp.float32
VM = pl.BlockSpec(memory_space=pltpu.VMEM)
SM = pl.BlockSpec(memory_space=pltpu.SMEM)
LIMIT = pltpu.CompilerParams(vmem_limit_bytes=24 * 1024 * 1024)
CORES, HOSTS, TP, SIDE = 2, 4, 8, 8
TOK, CAP = 8, 4


def iota(shape, dim):
    return lax.broadcasted_iota(jnp.int32, shape, dim)


def route_kernel(core_ref, both_ref, out_ref, mix_ref):
    core = core_ref[0]
    both = both_ref[...]
    lane = iota((1, 128), 1)
    meta = jnp.where(iota((8, 128), 1) < 16, both[8:16, 0:128], both[24:32, 0:128])
    real = (iota((8, 128), 1) % 16 < TOK) & (iota((8, 128), 1) < 32)
    meta = jnp.where(real, meta, -1.0)
    row = iota((32, 128), 0)
    expert = (2 * (row // 8) + core).astype(F32)
    group, place = (row // CAP) % 2, (row % CAP).astype(F32)
    inside = ((meta[0:1] == expert) | (meta[1:2] == expert)) & (iota((32, 128), 1) // 16 == group)
    inside = inside.astype(F32)
    before = (iota((128, 128), 0) < iota((128, 128), 1)).astype(BF)
    rank = jnp.dot(inside.astype(BF), before, preferred_element_type=F32)
    pick = jnp.where(rank == place, inside, 0.0).astype(BF)
    slots = jnp.dot(pick[:, 0:32], both.astype(BF), preferred_element_type=F32)
    for h in range(HOSTS):
        mine = slots[8 * h : 8 * h + 8].astype(BF)
        for t in range(TP):
            out_ref[TP * h + t] = mine
    columns = jnp.transpose(meta)[0:32]
    spot = iota((32, 256), 1)
    expert = (2 * (spot // 64) + core).astype(F32)
    group, place = (spot // CAP) % 2, (spot % CAP).astype(F32)
    first, second = columns[:, 0:1] == expert, columns[:, 1:2] == expert
    inside = ((first | second) & (iota((32, 256), 0) // 16 == group)).astype(F32)
    before = (iota((32, 32), 1) < iota((32, 32), 0)).astype(BF)
    rank = jnp.dot(before, inside.astype(BF), preferred_element_type=F32)
    weight = jnp.where(first, columns[:, 2:3], 0.0) + jnp.where(second, columns[:, 3:4], 0.0)
    mix = jnp.where((rank == place) & (inside > 0.0), weight, 0.0)
    high = mix.astype(BF)
    mix_ref[0:32] = high
    mix_ref[32:64] = (mix - high.astype(F32)).astype(BF)


def up_kernel(slots_ref, gate_ref, up_ref, out_ref):
    slots = slots_ref[...].reshape(256, 768)
    for pair in range(SIDE // 2):
        cols = slice(256 * pair, 256 * pair + 256)
        for half, ref in enumerate((gate_ref, up_ref)):
            part = jnp.dot(slots, ref[0, :, cols], preferred_element_type=F32).astype(BF)
            out_ref[2 * pair, :, 128 * half : 128 * half + 128] = part[:, 0:128]
            out_ref[2 * pair + 1, :, 128 * half : 128 * half + 128] = part[:, 128:256]


def hidden_kernel(parts_ref, out_ref):
    total = parts_ref[0].astype(F32)
    for s in range(1, SIDE):
        total = total + parts_ref[s].astype(F32)
    gate, up = total[:, 0:128], total[:, 128:256]
    hidden = (gate / (1.0 + jnp.exp(-gate)) * up).astype(BF)
    for s in range(SIDE):
        out_ref[s] = hidden


def down_kernel(hidden_ref, down_ref, out_ref):
    hidden = jnp.concatenate([hidden_ref[s] for s in range(SIDE)], axis=1)
    out = jnp.dot(hidden, down_ref[0], preferred_element_type=F32)
    out_ref[...] = out.astype(BF).reshape(32, 8, 768)


def mix_kernel(mix_ref, parts_ref, out_ref):
    both = jnp.dot(mix_ref[...], parts_ref[...].reshape(256, 768), preferred_element_type=F32)
    both = both[0:32] + both[32:64]
    out_ref[0] = both[0:8]
    out_ref[1] = both[16:24]


def local(rows, expert_ids, combine, w_gate, w_up, w_down):
    width = rows.shape[1]
    core = lax.axis_index("core").astype(jnp.int32)
    ids, weights = expert_ids.T.astype(F32), combine.T
    meta = jnp.concatenate([ids, weights, jnp.zeros((4, TOK), F32)], axis=0)
    meta = jnp.concatenate([meta, jnp.zeros((8, 8), F32), meta, jnp.zeros((8, width - 24), F32)], axis=1)
    mine = jnp.concatenate([rows.astype(F32), meta], axis=0)
    both = lax.all_gather(mine, "core", axis=0, tiled=True)
    slots, mix = pl.pallas_call(
        route_kernel,
        out_shape=(
            jax.ShapeDtypeStruct((32, 8, width), BF),
            jax.ShapeDtypeStruct((64, 256), BF),
        ),
        in_specs=[SM, VM],
        out_specs=(VM, VM),
        compiler_params=LIMIT,
    )(core.reshape(1), both)
    slots = lax.all_to_all(slots, ("host", "tp"), 0, 0, tiled=True)
    parts = pl.pallas_call(
        up_kernel,
        out_shape=jax.ShapeDtypeStruct((SIDE, 256, 256), BF),
        in_specs=[VM, VM, VM],
        out_specs=VM,
        compiler_params=LIMIT,
    )(slots, w_gate, w_up)
    parts = lax.all_to_all(parts, "side", 0, 0, tiled=True)
    hidden = pl.pallas_call(
        hidden_kernel,
        out_shape=jax.ShapeDtypeStruct((SIDE, 256, 128), BF),
        in_specs=[VM],
        out_specs=VM,
        compiler_params=LIMIT,
    )(parts)
    hidden = lax.all_to_all(hidden, "side", 0, 0, tiled=True)
    outs = pl.pallas_call(
        down_kernel,
        out_shape=jax.ShapeDtypeStruct((32, 8, width), BF),
        in_specs=[VM, VM],
        out_specs=VM,
        compiler_params=LIMIT,
    )(hidden, w_down)
    outs = lax.all_to_all(outs, ("host", "tp"), 0, 0, tiled=True)
    mixed = pl.pallas_call(
        mix_kernel,
        out_shape=jax.ShapeDtypeStruct((2, TOK, width), F32),
        in_specs=[VM, VM],
        out_specs=VM,
        compiler_params=LIMIT,
    )(mix, outs)
    mixed = lax.all_gather(mixed, "core", axis=0)
    mixed = lax.dynamic_index_in_dim(mixed, core, 1, False)
    return (mixed[0] + mixed[1]).astype(BF)


def solution(mesh):
    fine = Mesh(mesh.devices.reshape(SIDE, HOSTS, CORES, TP), ("side", "host", "core", "tp"))
    tokens = ("host", "core", "tp")
    experts = ("host", "core")
    return jax.shard_map(
        local,
        mesh=fine,
        in_specs=(
            P(tokens, "side"),
            P(tokens, None),
            P(tokens, None),
            P(experts, "side", "tp"),
            P(experts, "side", "tp"),
            P(experts, "tp", "side"),
        ),
        out_specs=P(tokens, "side"),
        check_vma=False,
    )
```

time: 237 us -> 97 us (0.41)
  waiting for transfers between devices: 165 us -> 12.8 us
  blocking collectives: 33.9 us -> 66.2 us
  between operations: 13.5 us -> 0.04 us
  matrix products: 7.7 us -> 0 us
  Pallas kernels: 0 us -> 2.97 us
  starting transfers between devices: 11.8 us -> 8.86 us
    psum x2 -> x0, waiting for transfers between devices: 158 us -> none  [the longest x1 79.4 us: local(): lax.psum(jnp.dot(hidden, down_local, preferred_element_type=jnp.float32)....]
    all_to_all x1 -> x3, blocking collectives: 33.9 us -> 51.7 us  [the longest x1 24.7 us: local(): slots = lax.all_to_all(slots, ('host', 'tp'), 0, 0, tiled=True)]
    all_gather x0 -> x2, blocking collectives: none -> 14.5 us  [the longest x1 8.4 us: local(): both = lax.all_gather(mine, 'core', axis=0, tiled=True)]
    dot_general x5 -> x0, matrix products: 7.7 us -> none  [the longest x1 3.25 us: local(): jnp.dot(hidden, down_local, preferred_element_type=jnp.float32)]
    all_to_all x1, waiting for transfers between devices: 7.16 us -> 12.8 us  [local(): outs = lax.all_to_all(outs, ('host', 'tp'), 0, 0, tiled=True)]
    pallas_call x0 -> x5, Pallas kernels: none -> 2.97 us  [the longest x1 1.32 us: local(): pl.pallas_call(down_kernel, out_shape=jax.ShapeDtypeStruct((32, 8, width)...]
    all_to_all x1, starting transfers between devices: 11.8 us -> 8.86 us  [local(): outs = lax.all_to_all(outs, ('host', 'tp'), 0, 0, tiled=True)]
    unnamed x8 -> x6, local copies, waits for them, and re-layouts: 0.02 us -> 2.82 us
  transfers between devices with their start and end apart: 3 -> 1, of which waited for: 3 -> 1; matrix products, arithmetic and copies ran while one was open for 0% -> 0% of each run, Pallas kernels for 0% -> 0%
where the time goes in v1:
time: 97 us; the launch traced here: 96.5 us
  blocking collectives  66.2 us (68%)
  waiting for transfers between devices  12.8 us (13%)
  starting transfers between devices  8.86 us (9%)
  Pallas kernels  2.97 us (3%)
  other arithmetic  2.83 us (3%)
  local copies, waits for them, and re-layouts  2.82 us (3%)
    all_to_all x1, blocking collectives, local(): slots = lax.all_to_all(slots, ('host', 'tp'), 0, 0, tiled=True)  24.7 us
    all_to_all x1, blocking collectives, local(): parts = lax.all_to_all(parts, 'side', 0, 0, tiled=True)  16 us
    all_to_all x1, waiting for transfers between devices, local(): outs = lax.all_to_all(outs, ('host', 'tp'), 0, 0, tiled=True)  12.8 us
    all_to_all x1, blocking collectives, local(): hidden = lax.all_to_all(hidden, 'side', 0, 0, tiled=True)  11 us
    all_to_all x1, starting transfers between devices, local(): outs = lax.all_to_all(outs, ('host', 'tp'), 0, 0, tiled=True)  8.86 us
    all_gather x1, blocking collectives, local(): both = lax.all_gather(mine, 'core', axis=0, tiled=True)  8.4 us
    all_gather x1, blocking collectives, local(): mixed = lax.all_gather(mixed, 'core', axis=0)  6.12 us
    unnamed x6, local copies, waits for them, and re-layouts  2.82 us
  transfers between devices with their start and end apart: 1, of which 1 were waited for; matrix products, arithmetic and copies ran while one was open for 0% of the time, Pallas kernels for 0%

profile of v1, /device:TPU:1, one launch (start us, length us, event | category | flops | bytes accessed | tf_op | source)
XLA Modules:
  0.0 96.5 jit_solution(13948248699079816255)
XLA Ops:
  0.0 0.7 convert_bitcast_fusion
  0.7 0.7 convert_element_type.15
  1.4 0.8 maximum_maximum_fusion
  2.2 8.4 %all_gather.9.both_ref = f32[32,768]{1,0:T(8,128)S(1)} all-gather(f32[16,768]{1,0:T(8,128)S(1)} %maximum_maximum_fusion), channel_id=1, replica_groups=mesh['side'=8,'host'=4,'core'=2,'tp'=8] {'core'}, dimensions={0}, use_global_device_ids=true | all-gather | bytes 147456 | tf_op jit(solution)/shard_map/all_gather | solution.py:98
  10.6 0.3 shard_map.64
  10.9 24.7 %all_to_all.20.slots_ref = bf16[32,8,768]{2,1,0:T(8,128)(2,1)S(1)} all-to-all(bf16[32,8,768]{2,1,0:T(8,128)(2,1)S(1)} %get-tuple-element.8), channel_id=1, replica_groups=mesh['side'=8,'host'=4,'core'=2,'tp'=8] {'host','tp'}, dimensions={0} | all-to-all | bytes 786432 | tf_op jit(solution)/shard_map/all_to_all | solution.py:109
  35.6 0.0 copy-start
  35.6 1.4 %copy-done = bf16[1,768,1024]{2,1,0:T(8,128)(2,1)S(1)} copy-done((bf16[1,768,1024]{2,1,0:T(8,128)(2,1)S(1)}, bf16[1,768,1024]{2,1,0:T(8,128)(2,1)}, u32[]{:S(2)}) %copy-start) | copy-done | bytes 1572888
  37.0 0.0 copy-start.1
  37.0 1.4 %copy-done.1 = bf16[1,768,1024]{2,1,0:T(8,128)(2,1)S(1)} copy-done((bf16[1,768,1024]{2,1,0:T(8,128)(2,1)S(1)}, bf16[1,768,1024]{2,1,0:T(8,128)(2,1)}, u32[]{:S(2)}) %copy-start.1) | copy-done | bytes 1572888
  38.4 1.0 %shard_map.65 = bf16[8,256,256]{2,1,0:T(8,128)(2,1)S(1)} custom-call(bf16[32,8,768]{2,1,0:T(8,128)(2,1)S(1)} %all_to_all.20.slots_ref, bf16[1,768,1024]{2,1,0:T(8,128)(2,1)S(1)} %copy-done, bf16[1,768,1024]{2,1,0:T(8,128)(2,1)S(1)} %copy-done.1), custom_call_target="tpu_custom_call" | custom-call | tf_op jit(solution)/shard_map/pallas_call | solution.py:110
  39.4 16.0 %all_to_all.21.parts_ref = bf16[8,256,256]{2,1,0:T(8,128)(2,1)S(1)} all-to-all(bf16[8,256,256]{2,1,0:T(8,128)(2,1)S(1)} %shard_map.65), channel_id=1, replica_groups=mesh['side'=8,'host'=4,'core'=2,'tp'=8] {'side'}, dimensions={0} | all-to-all | bytes 2097152 | tf_op jit(solution)/shard_map/all_to_all | solution.py:117
  55.5 0.0 copy-start.2
  55.5 0.2 shard_map.66
  55.7 11.0 %all_to_all.22.hidden_ref = bf16[8,256,128]{2,1,0:T(8,128)(2,1)S(1)} all-to-all(bf16[8,256,128]{2,1,0:T(8,128)(2,1)S(1)} %shard_map.66), channel_id=1, replica_groups=mesh['side'=8,'host'=4,'core'=2,'tp'=8] {'side'}, dimensions={0} | all-to-all | bytes 1048576 | tf_op jit(solution)/shard_map/all_to_all | solution.py:125
  66.6 0.0 copy-done.2
  66.6 1.3 %shard_map.67 = bf16[32,8,768]{2,1,0:T(8,128)(2,1)} custom-call(bf16[8,256,128]{2,1,0:T(8,128)(2,1)S(1)} %all_to_all.22.hidden_ref, bf16[1,1024,768]{2,1,0:T(8,128)(2,1)S(1)} %copy-done.2), custom_call_target="tpu_custom_call" | custom-call | tf_op jit(solution)/shard_map/pallas_call | solution.py:126
  67.9 8.9 %all-to-all-start.3 = ((bf16[32,8,768]{2,1,0:T(8,128)(2,1)}), bf16[32,8,768]{2,1,0:T(8,128)(2,1)S(1)}, u32[]{:S(2)}, u32[]{:S(2)}) async-start(bf16[32,8,768]{2,1,0:T(8,128)(2,1)} %shard_map.67), calls=%async_computation.3 | async-start | bytes 786432 | tf_op jit(solution)/shard_map/all_to_all | solution.py:133
  76.8 12.8 %all-to-all-done.3.parts_ref = bf16[32,8,768]{2,1,0:T(8,128)(2,1)S(1)} async-done(((bf16[32,8,768]{2,1,0:T(8,128)(2,1)}), bf16[32,8,768]{2,1,0:T(8,128)(2,1)S(1)}, u32[]{:S(2)}, u32[]{:S(2)}) %all-to-all-start.3) | async-done | bytes 393248 | tf_op jit(solution)/shard_map/all_to_all | solution.py:133
  89.6 0.2 shard_map.68
  89.8 6.1 %all-gather = f32[4,8,768]{2,1,0:T(8,128)S(1)} all-gather(f32[2,8,768]{2,1,0:T(8,128)S(1)} %shard_map.68), channel_id=2, replica_groups=mesh['side'=8,'host'=4,'core'=2,'tp'=8] {'core'}, dimensions={0}, use_global_device_ids=true | all-gather | bytes 147456 | tf_op jit(solution)/shard_map/all_gather | solution.py:141
  95.9 0.6 fusion.1
  (3 shorter events, 0.0 us)
Async XLA Ops:
  35.6 1.4 %copy-start = (bf16[1,768,1024]{2,1,0:T(8,128)(2,1)S(1)}, bf16[1,768,1024]{2,1,0:T(8,128)(2,1)}, u32[]{:S(2)}) copy-start(bf16[1,768,1024]{2,1,0:T(8,128)(2,1)} %gate_ref.1) | copy-start | bytes 4718596
  37.0 1.4 %copy-start.1 = (bf16[1,768,1024]{2,1,0:T(8,128)(2,1)S(1)}, bf16[1,768,1024]{2,1,0:T(8,128)(2,1)}, u32[]{:S(2)}) copy-start(bf16[1,768,1024]{2,1,0:T(8,128)(2,1)} %up_ref.1) | copy-start | bytes 4718596
  55.5 11.1 %copy-start.2 = (bf16[1,1024,768]{2,1,0:T(8,128)(2,1)S(1)}, bf16[1,1024,768]{2,1,0:T(8,128)(2,1)}, u32[]{:S(2)}) copy-start(bf16[1,1024,768]{2,1,0:T(8,128)(2,1)} %down_ref.1) | copy-start | bytes 4718596
  67.9 21.7 %all-to-all-start.3 = ((bf16[32,8,768]{2,1,0:T(8,128)(2,1)}), bf16[32,8,768]{2,1,0:T(8,128)(2,1)S(1)}, u32[]{:S(2)}, u32[]{:S(2)}) async-start(bf16[32,8,768]{2,1,0:T(8,128)(2,1)} %shard_map.67), calls=%async_computation.3 | async-start | bytes 786432 | tf_op jit(solution)/shard_map/all_to_all | solution.py:133

commit v2 on v1

--- a/solution.py
+++ b/solution.py
@@ -11,20 +11,35 @@
 BF, F32 = jnp.bfloat16, jnp.float32
 VM = pl.BlockSpec(memory_space=pltpu.VMEM)
 SM = pl.BlockSpec(memory_space=pltpu.SMEM)
+HBM = pl.BlockSpec(memory_space=pltpu.HBM)
 LIMIT = pltpu.CompilerParams(vmem_limit_bytes=24 * 1024 * 1024)
 CORES, HOSTS, TP, SIDE = 2, 4, 8, 8
 TOK, CAP = 8, 4
+
+
+def far(array):
+    return pltpu.with_memory_space_constraint(array, pltpu.HBM)
+
+
+def near(array):
+    return pltpu.with_memory_space_constraint(array, pltpu.VMEM)
 
 
 def iota(shape, dim):
     return lax.broadcasted_iota(jnp.int32, shape, dim)
 
 
-def route_kernel(core_ref, both_ref, out_ref, mix_ref):
+def pack_kernel(rows_ref, ids_ref, weights_ref, out_ref):
+    out_ref[0:8] = rows_ref[...].astype(F32)
+    out_ref[8:16] = jnp.zeros((8, out_ref.shape[1]), F32)
+    out_ref[8:10, 0:TOK] = ids_ref[...].astype(F32)
+    out_ref[10:12, 0:TOK] = weights_ref[...]
+
+
+def route_kernel(core_ref, both_ref, gate_hbm, up_hbm, out_ref, mix_ref):
     core = core_ref[0]
     both = both_ref[...]
-    lane = iota((1, 128), 1)
-    meta = jnp.where(iota((8, 128), 1) < 16, both[8:16, 0:128], both[24:32, 0:128])
+    meta = jnp.where(iota((8, 128), 1) < 16, both[8:16, 0:128], pltpu.roll(both[24:32, 0:128], 16, 1))
     real = (iota((8, 128), 1) % 16 < TOK) & (iota((8, 128), 1) < 32)
     meta = jnp.where(real, meta, -1.0)
     row = iota((32, 128), 0)
@@ -88,13 +103,21 @@
     out_ref[1] = both[16:24]
 
 
+def add_kernel(core_ref, both_ref, out_ref):
+    core = core_ref[0]
+    out_ref[...] = (both_ref[core] + both_ref[2 + core]).astype(BF)
+
+
 def local(rows, expert_ids, combine, w_gate, w_up, w_down):
     width = rows.shape[1]
-    core = lax.axis_index("core").astype(jnp.int32)
-    ids, weights = expert_ids.T.astype(F32), combine.T
-    meta = jnp.concatenate([ids, weights, jnp.zeros((4, TOK), F32)], axis=0)
-    meta = jnp.concatenate([meta, jnp.zeros((8, 8), F32), meta, jnp.zeros((8, width - 24), F32)], axis=1)
-    mine = jnp.concatenate([rows.astype(F32), meta], axis=0)
+    core = lax.axis_index("core").astype(jnp.int32).reshape(1)
+    mine = pl.pallas_call(
+        pack_kernel,
+        out_shape=jax.ShapeDtypeStruct((16, width), F32),
+        in_specs=[VM, VM, VM],
+        out_specs=VM,
+        compiler_params=LIMIT,
+    )(far(rows), far(expert_ids.T), far(combine.T))
     both = lax.all_gather(mine, "core", axis=0, tiled=True)
     slots, mix = pl.pallas_call(
         route_kernel,
@@ -102,10 +125,10 @@
             jax.ShapeDtypeStruct((32, 8, width), BF),
             jax.ShapeDtypeStruct((64, 256), BF),
         ),
-        in_specs=[SM, VM],
+        in_specs=[SM, VM, HBM, HBM],
         out_specs=(VM, VM),
         compiler_params=LIMIT,
-    )(core.reshape(1), both)
+    )(core, both, far(w_gate), far(w_up))
     slots = lax.all_to_all(slots, ("host", "tp"), 0, 0, tiled=True)
     parts = pl.pallas_call(
         up_kernel,
@@ -113,7 +136,7 @@
         in_specs=[VM, VM, VM],
         out_specs=VM,
         compiler_params=LIMIT,
-    )(slots, w_gate, w_up)
+    )(slots, near(w_gate), near(w_up))
     parts = lax.all_to_all(parts, "side", 0, 0, tiled=True)
     hidden = pl.pallas_call(
         hidden_kernel,
@@ -138,9 +161,14 @@
         out_specs=VM,
         compiler_params=LIMIT,
     )(mix, outs)
-    mixed = lax.all_gather(mixed, "core", axis=0)
-    mixed = lax.dynamic_index_in_dim(mixed, core, 1, False)
-    return (mixed[0] + mixed[1]).astype(BF)
+    mixed = lax.all_gather(mixed, "core", axis=0, tiled=True)
+    return pl.pallas_call(
+        add_kernel,
+        out_shape=jax.ShapeDtypeStruct((TOK, width), BF),
+        in_specs=[SM, VM],
+        out_specs=VM,
+        compiler_params=LIMIT,
+    )(core, mixed)
 
 
 def solution(mesh):

time: 97 us -> 91.8 us (0.946)
  blocking collectives: 66.2 us -> 87.8 us
  waiting for transfers between devices: 12.8 us -> 0 us
  starting transfers between devices: 8.86 us -> 0 us
  other arithmetic: 2.83 us -> 0 us
  local copies, waits for them, and re-layouts: 2.82 us -> 0.01 us
    all_to_all x0 -> x1, blocking collectives: none -> 21.5 us  [local(): outs = lax.all_to_all(outs, ('host', 'tp'), 0, 0, tiled=True)]
    all_to_all x1 -> x0, waiting for transfers between devices: 12.8 us -> none  [local(): outs = lax.all_to_all(outs, ('host', 'tp'), 0, 0, tiled=True)]
    all_to_all x1 -> x0, starting transfers between devices: 8.86 us -> none  [local(): outs = lax.all_to_all(outs, ('host', 'tp'), 0, 0, tiled=True)]
    unnamed x6, local copies, waits for them, and re-layouts: 2.82 us -> 0.01 us
    convert_element_type x3 -> x0, other arithmetic: 1.99 us -> none  [the longest x1 0.71 us: local(): mine = jnp.concatenate([rows.astype(F32), meta], axis=0)]
    pallas_call x0 -> x2, Pallas kernels: none -> 1.33 us  [the longest x1 0.73 us: local(): pl.pallas_call(pack_kernel, out_shape=jax.ShapeDtypeStruct((16, width), F...]
  transfers between devices with their start and end apart: 1 -> 0, of which waited for: 1 -> 0; matrix products, arithmetic and copies ran while one was open for 0% -> 0% of each run, Pallas kernels for 0% -> 0%
where the time goes in v2:
time: 91.8 us; the launch traced here: 91.5 us
  blocking collectives  87.8 us (96%)
  Pallas kernels  3.63 us (4%)
    all_to_all x1, blocking collectives, local(): slots = lax.all_to_all(slots, ('host', 'tp'), 0, 0, tiled=True)  24.8 us
    all_to_all x1, blocking collectives, local(): outs = lax.all_to_all(outs, ('host', 'tp'), 0, 0, tiled=True)  21.5 us
    all_to_all x1, blocking collectives, local(): parts = lax.all_to_all(parts, 'side', 0, 0, tiled=True)  16 us
    all_to_all x1, blocking collectives, local(): hidden = lax.all_to_all(hidden, 'side', 0, 0, tiled=True)  11 us
    all_gather x1, blocking collectives, local(): both = lax.all_gather(mine, 'core', axis=0, tiled=True)  8.39 us
    all_gather x1, blocking collectives, local(): mixed = lax.all_gather(mixed, 'core', axis=0, tiled=True)  6.1 us

profile of v2, /device:TPU:1, one launch (start us, length us, event | category | flops | bytes accessed | tf_op | source)
XLA Modules:
  0.0 91.5 jit_solution(10871854942758825127)
XLA Ops:
  0.0 0.7 shard_map.64
  0.7 8.4 %all_gather.6.both_ref = f32[32,768]{1,0:T(8,128)S(1)} all-gather(f32[16,768]{1,0:T(8,128)S(1)} %shard_map.64), channel_id=1, replica_groups=mesh['side'=8,'host'=4,'core'=2,'tp'=8] {'core'}, dimensions={0}, use_global_device_ids=true | all-gather | bytes 147456 | tf_op jit(solution)/shard_map/all_gather | solution.py:121
  9.1 0.0 copy-start
  9.1 0.0 copy-start.1
  9.1 0.4 shard_map.65
  9.5 24.8 %all_to_all.20.slots_ref = bf16[32,8,768]{2,1,0:T(8,128)(2,1)S(1)} all-to-all(bf16[32,8,768]{2,1,0:T(8,128)(2,1)S(1)} %get-tuple-element.8), channel_id=1, replica_groups=mesh['side'=8,'host'=4,'core'=2,'tp'=8] {'host','tp'}, dimensions={0} | all-to-all | bytes 786432 | tf_op jit(solution)/shard_map/all_to_all | solution.py:132
  34.3 0.0 copy-done
  34.3 0.0 copy-done.1
  34.3 1.0 %shard_map.66 = bf16[8,256,256]{2,1,0:T(8,128)(2,1)S(1)} custom-call(bf16[32,8,768]{2,1,0:T(8,128)(2,1)S(1)} %all_to_all.20.slots_ref, bf16[1,768,1024]{2,1,0:T(8,128)(2,1)S(1)} %copy-done, bf16[1,768,1024]{2,1,0:T(8,128)(2,1)S(1)} %copy-done.1), custom_call_target="tpu_custom_call" | custom-call | tf_op jit(solution)/shard_map/pallas_call | solution.py:133
  35.3 16.0 %all_to_all.21.parts_ref = bf16[8,256,256]{2,1,0:T(8,128)(2,1)S(1)} all-to-all(bf16[8,256,256]{2,1,0:T(8,128)(2,1)S(1)} %shard_map.66), channel_id=1, replica_groups=mesh['side'=8,'host'=4,'core'=2,'tp'=8] {'side'}, dimensions={0} | all-to-all | bytes 2097152 | tf_op jit(solution)/shard_map/all_to_all | solution.py:140
  51.3 0.0 copy-start.2
  51.3 0.2 shard_map.67
  51.5 11.0 %all_to_all.22.hidden_ref = bf16[8,256,128]{2,1,0:T(8,128)(2,1)S(1)} all-to-all(bf16[8,256,128]{2,1,0:T(8,128)(2,1)S(1)} %shard_map.67), channel_id=1, replica_groups=mesh['side'=8,'host'=4,'core'=2,'tp'=8] {'side'}, dimensions={0} | all-to-all | bytes 1048576 | tf_op jit(solution)/shard_map/all_to_all | solution.py:148
  62.5 0.0 copy-done.2
  62.5 0.6 shard_map.68
  63.1 21.5 %all_to_all.23.parts_ref = bf16[32,8,768]{2,1,0:T(8,128)(2,1)S(1)} all-to-all(bf16[32,8,768]{2,1,0:T(8,128)(2,1)S(1)} %shard_map.68), channel_id=1, replica_groups=mesh['side'=8,'host'=4,'core'=2,'tp'=8] {'host','tp'}, dimensions={0} | all-to-all | bytes 786432 | tf_op jit(solution)/shard_map/all_to_all | solution.py:156
  84.6 0.2 shard_map.69
  84.8 6.1 %all_gather.7.both_ref = f32[4,8,768]{2,1,0:T(8,128)S(1)} all-gather(f32[2,8,768]{2,1,0:T(8,128)S(1)} %shard_map.69), channel_id=1, replica_groups=mesh['side'=8,'host'=4,'core'=2,'tp'=8] {'core'}, dimensions={0}, use_global_device_ids=true | all-gather | bytes 147456 | tf_op jit(solution)/shard_map/all_gather | solution.py:164
  90.9 0.6 shard_map.70
Async XLA Ops:
  9.1 25.2 %copy-start = (bf16[1,768,1024]{2,1,0:T(8,128)(2,1)S(1)}, bf16[1,768,1024]{2,1,0:T(8,128)(2,1)}, u32[]{:S(2)}) copy-start(bf16[1,768,1024]{2,1,0:T(8,128)(2,1)} %gate_ref.1) | copy-start | bytes 4718596
  9.1 25.2 %copy-start.1 = (bf16[1,768,1024]{2,1,0:T(8,128)(2,1)S(1)}, bf16[1,768,1024]{2,1,0:T(8,128)(2,1)}, u32[]{:S(2)}) copy-start(bf16[1,768,1024]{2,1,0:T(8,128)(2,1)} %up_ref.1) | copy-start | bytes 4718596
  51.3 11.2 %copy-start.2 = (bf16[1,1024,768]{2,1,0:T(8,128)(2,1)S(1)}, bf16[1,1024,768]{2,1,0:T(8,128)(2,1)}, u32[]{:S(2)}) copy-start(bf16[1,1024,768]{2,1,0:T(8,128)(2,1)} %down_ref.1) | copy-start | bytes 4718596

commit v3 on v2

--- a/solution.py
+++ b/solution.py
@@ -15,6 +15,8 @@
 LIMIT = pltpu.CompilerParams(vmem_limit_bytes=24 * 1024 * 1024)
 CORES, HOSTS, TP, SIDE = 2, 4, 8, 8
 TOK, CAP = 8, 4
+FEW = 128
+EMPTY = 64.0
 
 
 def far(array):
@@ -49,8 +51,10 @@
     inside = inside.astype(F32)
     before = (iota((128, 128), 0) < iota((128, 128), 1)).astype(BF)
     rank = jnp.dot(inside.astype(BF), before, preferred_element_type=F32)
-    pick = jnp.where(rank == place, inside, 0.0).astype(BF)
-    slots = jnp.dot(pick[:, 0:32], both.astype(BF), preferred_element_type=F32)
+    pick = jnp.where(rank == place, inside, 0.0)
+    slots = jnp.dot(pick.astype(BF)[:, 0:32], both.astype(BF), preferred_element_type=F32)
+    empty = 1.0 - jnp.sum(pick, axis=1, keepdims=True)
+    slots = slots + jnp.where(iota(slots.shape, 1) == 0, EMPTY * empty, 0.0)
     for h in range(HOSTS):
         mine = slots[8 * h : 8 * h + 8].astype(BF)
         for t in range(TP):
@@ -70,8 +74,20 @@
     mix_ref[32:64] = (mix - high.astype(F32)).astype(BF)
 
 
-def up_kernel(slots_ref, gate_ref, up_ref, out_ref):
+def up_kernel(slots_ref, gate_ref, up_ref, down_hbm, out_ref, spread_ref, count_ref):
     slots = slots_ref[...].reshape(256, 768)
+    used = (slots[:, 0:1].astype(F32) < EMPTY / 2).astype(F32)
+    count_ref[0] = jnp.sum(used).astype(jnp.int32)
+    wide = jnp.broadcast_to(used, (256, 256))
+    row, col = iota((256, 256), 0), iota((256, 256), 1)
+    ones = jnp.ones((8, 256), BF)
+    rank = jnp.dot(ones, jnp.where(row < col, wide, 0.0).astype(BF), preferred_element_type=F32)[0:1]
+    here = jnp.dot(ones, jnp.where(row == col, wide, 0.0).astype(BF), preferred_element_type=F32)[0:1]
+    front = jnp.where(row.astype(F32) == rank, here, 0.0).astype(BF)
+    slots = jnp.dot(front, slots, preferred_element_type=F32).astype(BF)
+    before = jnp.where(col < row, 1.0, 0.0).astype(BF)
+    rank = jnp.dot(before, wide.astype(BF), preferred_element_type=F32)
+    spread_ref[...] = jnp.where(rank == col.astype(F32), wide, 0.0).astype(BF)
     for pair in range(SIDE // 2):
         cols = slice(256 * pair, 256 * pair + 256)
         for half, ref in enumerate((gate_ref, up_ref)):
@@ -90,9 +106,10 @@
         out_ref[s] = hidden
 
 
-def down_kernel(hidden_ref, down_ref, out_ref):
+def down_kernel(hidden_ref, spread_ref, down_ref, out_ref):
     hidden = jnp.concatenate([hidden_ref[s] for s in range(SIDE)], axis=1)
-    out = jnp.dot(hidden, down_ref[0], preferred_element_type=F32)
+    out = jnp.dot(hidden, down_ref[0], preferred_element_type=F32).astype(BF)
+    out = jnp.dot(spread_ref[...], out, preferred_element_type=F32)
     out_ref[...] = out.astype(BF).reshape(32, 8, 768)
 
 
@@ -106,6 +123,23 @@
 def add_kernel(core_ref, both_ref, out_ref):
     core = core_ref[0]
     out_ref[...] = (both_ref[core] + both_ref[2 + core]).astype(BF)
+
+
+def middle(parts):
+    parts = lax.all_to_all(parts, "side", 0, 0, tiled=True)
+    hidden = pl.pallas_call(
+        hidden_kernel,
+        out_shape=jax.ShapeDtypeStruct(parts.shape[:2] + (128,), BF),
+        in_specs=[VM],
+        out_specs=VM,
+        compiler_params=LIMIT,
+    )(parts)
+    return lax.all_to_all(hidden, "side", 0, 0, tiled=True)
+
+
+def few(parts):
+    hidden = middle(parts[:, :FEW])
+    return jnp.pad(hidden, ((0, 0), (0, 256 - FEW), (0, 0)))
 
 
 def local(rows, expert_ids, combine, w_gate, w_up, w_down):
@@ -130,29 +164,25 @@
         compiler_params=LIMIT,
     )(core, both, far(w_gate), far(w_up))
     slots = lax.all_to_all(slots, ("host", "tp"), 0, 0, tiled=True)
-    parts = pl.pallas_call(
+    parts, spread, count = pl.pallas_call(
         up_kernel,
-        out_shape=jax.ShapeDtypeStruct((SIDE, 256, 256), BF),
-        in_specs=[VM, VM, VM],
-        out_specs=VM,
-        compiler_params=LIMIT,
-    )(slots, near(w_gate), near(w_up))
-    parts = lax.all_to_all(parts, "side", 0, 0, tiled=True)
-    hidden = pl.pallas_call(
-        hidden_kernel,
-        out_shape=jax.ShapeDtypeStruct((SIDE, 256, 128), BF),
-        in_specs=[VM],
-        out_specs=VM,
-        compiler_params=LIMIT,
-    )(parts)
-    hidden = lax.all_to_all(hidden, "side", 0, 0, tiled=True)
+        out_shape=(
+            jax.ShapeDtypeStruct((SIDE, 256, 256), BF),
+            jax.ShapeDtypeStruct((256, 256), BF),
+            jax.ShapeDtypeStruct((1,), jnp.int32),
+        ),
+        in_specs=[VM, VM, VM, HBM],
+        out_specs=(VM, VM, SM),
+        compiler_params=LIMIT,
+    )(slots, near(w_gate), near(w_up), far(w_down))
+    hidden = lax.cond(count[0] <= FEW, few, middle, parts)
     outs = pl.pallas_call(
         down_kernel,
         out_shape=jax.ShapeDtypeStruct((32, 8, width), BF),
-        in_specs=[VM, VM],
-        out_specs=VM,
-        compiler_params=LIMIT,
-    )(hidden, w_down)
+        in_specs=[VM, VM, VM],
+        out_specs=VM,
+        compiler_params=LIMIT,
+    )(hidden, spread, near(w_down))
     outs = lax.all_to_all(outs, ("host", "tp"), 0, 0, tiled=True)
     mixed = pl.pallas_call(
         mix_kernel,

time: 91.8 us -> 91.3 us (level)
  blocking collectives: 87.8 us -> 86.3 us
  Pallas kernels: 3.63 us -> 4.6 us
    all_to_all x1, blocking collectives: 21.5 us -> 30.3 us  [local(): outs = lax.all_to_all(outs, ('host', 'tp'), 0, 0, tiled=True)]
    all_to_all x2, blocking collectives: 27 us -> 19.9 us  [the longest x1 11.4 us: middle(): parts = lax.all_to_all(parts, 'side', 0, 0, tiled=True)]
    all_gather x1, blocking collectives: 6.1 us -> 2.85 us  [local(): mixed = lax.all_gather(mixed, 'core', axis=0, tiled=True)]
where the time goes in v3:
time: 91.3 us; the launch traced here: 91.7 us
  blocking collectives  86.3 us (95%)
  Pallas kernels  4.6 us (5%)
    all_to_all x1, blocking collectives, local(): outs = lax.all_to_all(outs, ('host', 'tp'), 0, 0, tiled=True)  30.3 us
    all_to_all x1, blocking collectives, local(): slots = lax.all_to_all(slots, ('host', 'tp'), 0, 0, tiled=True)  24.8 us
    all_to_all x1, blocking collectives, middle(): parts = lax.all_to_all(parts, 'side', 0, 0, tiled=True)  11.4 us
    all_to_all x1, blocking collectives, middle(): return lax.all_to_all(hidden, 'side', 0, 0, tiled=True)  8.49 us
    all_gather x1, blocking collectives, local(): both = lax.all_gather(mine, 'core', axis=0, tiled=True)  8.39 us
    all_gather x1, blocking collectives, local(): mixed = lax.all_gather(mixed, 'core', axis=0, tiled=True)  2.85 us

profile of v3, /device:TPU:1, one launch (start us, length us, event | category | flops | bytes accessed | tf_op | source)
XLA Modules:
  0.0 91.7 jit_solution(8393814633383547334)
XLA Ops:
  0.0 0.7 shard_map.64
  0.7 8.4 %all_gather.6.both_ref = f32[32,768]{1,0:T(8,128)S(1)} all-gather(f32[16,768]{1,0:T(8,128)S(1)} %shard_map.64), channel_id=1, replica_groups=mesh['side'=8,'host'=4,'core'=2,'tp'=8] {'core'}, dimensions={0}, use_global_device_ids=true | all-gather | bytes 147456 | tf_op jit(solution)/shard_map/all_gather | solution.py:155
  9.1 0.0 copy-start.1
  9.1 0.0 copy-start.2
  9.1 0.4 shard_map.65
  9.5 24.8 %all_to_all.30.slots_ref = bf16[32,8,768]{2,1,0:T(8,128)(2,1)S(1)} all-to-all(bf16[32,8,768]{2,1,0:T(8,128)(2,1)S(1)} %get-tuple-element.16), channel_id=1, replica_groups=mesh['side'=8,'host'=4,'core'=2,'tp'=8] {'host','tp'}, dimensions={0} | all-to-all | bytes 786432 | tf_op jit(solution)/shard_map/all_to_all | solution.py:166
  34.3 0.0 copy-done.1
  34.3 0.0 copy-done.2
  34.3 1.8 %shard_map.66 = (bf16[8,256,256]{2,1,0:T(8,128)(2,1)S(1)}, bf16[256,256]{1,0:T(8,128)(2,1)S(1)}, s32[1]{0:T(128)}) custom-call(bf16[32,8,768]{2,1,0:T(8,128)(2,1)S(1)} %all_to_all.30.slots_ref, bf16[1,768,1024]{2,1,0:T(8,128)(2,1)S(1)} %copy-done.1, bf16[1,768,1024]{2,1,0:T(8,128)(2,1)S(1)} %copy-done.2, bf16[1,1024,768]{2,1,0:T(8,128)(2,1)} %down_ref.1), custom_call_target="tpu_custom_call" | custom-call | tf_op jit(solution)/shard_map/pallas_call | solution.py:167
  36.7 0.0 copy-start
  36.7 20.1 %conditional.1 = (bf16[8,256,128]{2,1,0:T(8,128)(2,1)S(1)}) conditional(s32[]{:T(128)} %bitcast.3, bf16[8,256,256]{2,1,0:T(8,128)(2,1)S(1)} %get-tuple-element.18, bf16[8,256,256]{2,1,0:T(8,128)(2,1)S(1)} %get-tuple-element.18), branch_computations={%region_0.0_spmd, %region_1.2_spmd} | conditional | bytes 3407882 | solution.py:178
  36.8 11.4 %all_to_all.28.parts_ref = bf16[8,128,256]{2,1,0:T(8,128)(2,1)S(1)} all-to-all(bf16[8,128,256]{2,1,0:T(8,128)(2,1)S(1)} %slice.2), channel_id=1, replica_groups=mesh['side'=8,'host'=4,'core'=2,'tp'=8] {'side'}, dimensions={0} | all-to-all | bytes 1048576 | tf_op jit(solution)/shard_map/cond/branch_1_fun/all_to_all | solution.py:129
  48.2 0.1 branch_1_fun.1
  48.3 8.5 %all_to_all.29 = bf16[8,128,128]{2,1,0:T(8,128)(2,1)S(1)} all-to-all(bf16[8,128,128]{2,1,0:T(8,128)(2,1)S(1)} %branch_1_fun.1), channel_id=1, replica_groups=mesh['side'=8,'host'=4,'core'=2,'tp'=8] {'side'}, dimensions={0} | all-to-all | bytes 524288 | tf_op jit(solution)/shard_map/cond/branch_1_fun/all_to_all | solution.py:137
  56.8 0.1 pad.3
  56.9 0.0 copy-done
  56.9 0.9 shard_map.67
  57.8 30.3 %all_to_all.31.parts_ref = bf16[32,8,768]{2,1,0:T(8,128)(2,1)S(1)} all-to-all(bf16[32,8,768]{2,1,0:T(8,128)(2,1)S(1)} %shard_map.67), channel_id=1, replica_groups=mesh['side'=8,'host'=4,'core'=2,'tp'=8] {'host','tp'}, dimensions={0} | all-to-all | bytes 786432 | tf_op jit(solution)/shard_map/all_to_all | solution.py:186
  88.1 0.2 shard_map.68
  88.3 2.8 %all_gather.7.both_ref = f32[4,8,768]{2,1,0:T(8,128)S(1)} all-gather(f32[2,8,768]{2,1,0:T(8,128)S(1)} %shard_map.68), channel_id=1, replica_groups=mesh['side'=8,'host'=4,'core'=2,'tp'=8] {'core'}, dimensions={0}, use_global_device_ids=true | all-gather | bytes 147456 | tf_op jit(solution)/shard_map/all_gather | solution.py:194
  91.1 0.6 shard_map.69
  (1 shorter events, 0.0 us)
Async XLA Ops:
  9.1 25.2 %copy-start.1 = (bf16[1,768,1024]{2,1,0:T(8,128)(2,1)S(1)}, bf16[1,768,1024]{2,1,0:T(8,128)(2,1)}, u32[]{:S(2)}) copy-start(bf16[1,768,1024]{2,1,0:T(8,128)(2,1)} %gate_ref.1) | copy-start | bytes 4718596
  9.1 25.2 %copy-start.2 = (bf16[1,768,1024]{2,1,0:T(8,128)(2,1)S(1)}, bf16[1,768,1024]{2,1,0:T(8,128)(2,1)}, u32[]{:S(2)}) copy-start(bf16[1,768,1024]{2,1,0:T(8,128)(2,1)} %up_ref.1) | copy-start | bytes 4718596
  36.7 20.2 %copy-start = (bf16[1,1024,768]{2,1,0:T(8,128)(2,1)S(1)}, bf16[1,1024,768]{2,1,0:T(8,128)(2,1)}, u32[]{:S(2)}) copy-start(bf16[1,1024,768]{2,1,0:T(8,128)(2,1)} %down_ref.1) | copy-start | bytes 4718596

commit v4 on v3

--- a/solution.py
+++ b/solution.py
@@ -74,26 +74,42 @@
     mix_ref[32:64] = (mix - high.astype(F32)).astype(BF)
 
 
-def up_kernel(slots_ref, gate_ref, up_ref, down_hbm, out_ref, spread_ref, count_ref):
-    slots = slots_ref[...].reshape(256, 768)
-    used = (slots[:, 0:1].astype(F32) < EMPTY / 2).astype(F32)
-    count_ref[0] = jnp.sum(used).astype(jnp.int32)
+def places(used):
     wide = jnp.broadcast_to(used, (256, 256))
     row, col = iota((256, 256), 0), iota((256, 256), 1)
     ones = jnp.ones((8, 256), BF)
     rank = jnp.dot(ones, jnp.where(row < col, wide, 0.0).astype(BF), preferred_element_type=F32)[0:1]
     here = jnp.dot(ones, jnp.where(row == col, wide, 0.0).astype(BF), preferred_element_type=F32)[0:1]
-    front = jnp.where(row.astype(F32) == rank, here, 0.0).astype(BF)
-    slots = jnp.dot(front, slots, preferred_element_type=F32).astype(BF)
+    front = jnp.where(row[0:FEW].astype(F32) == rank, here, 0.0).astype(BF)
     before = jnp.where(col < row, 1.0, 0.0).astype(BF)
-    rank = jnp.dot(before, wide.astype(BF), preferred_element_type=F32)
-    spread_ref[...] = jnp.where(rank == col.astype(F32), wide, 0.0).astype(BF)
-    for pair in range(SIDE // 2):
-        cols = slice(256 * pair, 256 * pair + 256)
-        for half, ref in enumerate((gate_ref, up_ref)):
-            part = jnp.dot(slots, ref[0, :, cols], preferred_element_type=F32).astype(BF)
-            out_ref[2 * pair, :, 128 * half : 128 * half + 128] = part[:, 0:128]
-            out_ref[2 * pair + 1, :, 128 * half : 128 * half + 128] = part[:, 128:256]
+    rank = jnp.dot(before, wide.astype(BF)[:, 0:FEW], preferred_element_type=F32)
+    spread = jnp.where(rank == col[:, 0:FEW].astype(F32), wide[:, 0:FEW], 0.0).astype(BF)
+    return front, spread
+
+
+def up_kernel(slots_ref, gate_ref, up_ref, down_hbm, out_ref, few_ref, spread_ref, count_ref):
+    slots = slots_ref[...].reshape(256, 768)
+    used = (slots[:, 0:1].astype(F32) < EMPTY / 2).astype(F32)
+    count = jnp.sum(used).astype(jnp.int32)
+    count_ref[0] = count
+
+    def parts(slots, ref_out):
+        for pair in range(SIDE // 2):
+            cols = slice(256 * pair, 256 * pair + 256)
+            for half, ref in enumerate((gate_ref, up_ref)):
+                part = jnp.dot(slots, ref[0, :, cols], preferred_element_type=F32).astype(BF)
+                ref_out[2 * pair, :, 128 * half : 128 * half + 128] = part[:, 0:128]
+                ref_out[2 * pair + 1, :, 128 * half : 128 * half + 128] = part[:, 128:256]
+
+    @pl.when(count > FEW)
+    def _():
+        parts(slots, out_ref)
+
+    @pl.when(count <= FEW)
+    def _():
+        front, spread = places(used)
+        spread_ref[...] = spread
+        parts(jnp.dot(front, slots, preferred_element_type=F32).astype(BF), few_ref)
 
 
 def hidden_kernel(parts_ref, out_ref):
@@ -106,10 +122,14 @@
         out_ref[s] = hidden
 
 
-def down_kernel(hidden_ref, spread_ref, down_ref, out_ref):
+def back_kernel(spread_ref, hidden_ref, out_ref):
+    for s in range(SIDE):
+        out_ref[s] = jnp.dot(spread_ref[...], hidden_ref[s], preferred_element_type=F32).astype(BF)
+
+
+def down_kernel(hidden_ref, down_ref, out_ref):
     hidden = jnp.concatenate([hidden_ref[s] for s in range(SIDE)], axis=1)
-    out = jnp.dot(hidden, down_ref[0], preferred_element_type=F32).astype(BF)
-    out = jnp.dot(spread_ref[...], out, preferred_element_type=F32)
+    out = jnp.dot(hidden, down_ref[0], preferred_element_type=F32)
     out_ref[...] = out.astype(BF).reshape(32, 8, 768)
 
 
@@ -137,9 +157,18 @@
     return lax.all_to_all(hidden, "side", 0, 0, tiled=True)
 
 
-def few(parts):
-    hidden = middle(parts[:, :FEW])
-    return jnp.pad(hidden, ((0, 0), (0, 256 - FEW), (0, 0)))
+def many(parts, few_parts, spread):
+    return middle(parts)
+
+
+def few(parts, few_parts, spread):
+    return pl.pallas_call(
+        back_kernel,
+        out_shape=jax.ShapeDtypeStruct((SIDE, 256, 128), BF),
+        in_specs=[VM, VM],
+        out_specs=VM,
+        compiler_params=LIMIT,
+    )(spread, middle(few_parts))
 
 
 def local(rows, expert_ids, combine, w_gate, w_up, w_down):
@@ -164,25 +193,26 @@
         compiler_params=LIMIT,
     )(core, both, far(w_gate), far(w_up))
     slots = lax.all_to_all(slots, ("host", "tp"), 0, 0, tiled=True)
-    parts, spread, count = pl.pallas_call(
+    parts, few_parts, spread, count = pl.pallas_call(
         up_kernel,
         out_shape=(
             jax.ShapeDtypeStruct((SIDE, 256, 256), BF),
-            jax.ShapeDtypeStruct((256, 256), BF),
+            jax.ShapeDtypeStruct((SIDE, FEW, 256), BF),
+            jax.ShapeDtypeStruct((256, FEW), BF),
             jax.ShapeDtypeStruct((1,), jnp.int32),
         ),
         in_specs=[VM, VM, VM, HBM],
-        out_specs=(VM, VM, SM),
+        out_specs=(VM, VM, VM, SM),
         compiler_params=LIMIT,
     )(slots, near(w_gate), near(w_up), far(w_down))
-    hidden = lax.cond(count[0] <= FEW, few, middle, parts)
+    hidden = lax.cond(count[0] <= FEW, few, many, parts, few_parts, spread)
     outs = pl.pallas_call(
         down_kernel,
         out_shape=jax.ShapeDtypeStruct((32, 8, width), BF),
-        in_specs=[VM, VM, VM],
-        out_specs=VM,
-        compiler_params=LIMIT,
-    )(hidden, spread, near(w_down))
+        in_specs=[VM, VM],
+        out_specs=VM,
+        compiler_params=LIMIT,
+    )(hidden, near(w_down))
     outs = lax.all_to_all(outs, ("host", "tp"), 0, 0, tiled=True)
     mixed = pl.pallas_call(
         mix_kernel,

time: 91.3 us -> 91.9 us (level)
  blocking collectives: 86.3 us -> 87.5 us
    all_to_all x1, blocking collectives: 30.3 us -> 31.5 us  [local(): outs = lax.all_to_all(outs, ('host', 'tp'), 0, 0, tiled=True)]
where the time goes in v4:
time: 91.9 us; the launch traced here: 92.7 us
  blocking collectives  87.5 us (95%)
  Pallas kernels  4.43 us (5%)
    all_to_all x1, blocking collectives, local(): outs = lax.all_to_all(outs, ('host', 'tp'), 0, 0, tiled=True)  31.5 us
    all_to_all x1, blocking collectives, local(): slots = lax.all_to_all(slots, ('host', 'tp'), 0, 0, tiled=True)  24.8 us
    all_to_all x1, blocking collectives, middle(): parts = lax.all_to_all(parts, 'side', 0, 0, tiled=True)  11.4 us
    all_to_all x1, blocking collectives, middle(): return lax.all_to_all(hidden, 'side', 0, 0, tiled=True)  8.49 us
    all_gather x1, blocking collectives, local(): both = lax.all_gather(mine, 'core', axis=0, tiled=True)  8.39 us
    all_gather x1, blocking collectives, local(): mixed = lax.all_gather(mixed, 'core', axis=0, tiled=True)  2.83 us

profile of v4, /device:TPU:1, one launch (start us, length us, event | category | flops | bytes accessed | tf_op | source)
XLA Modules:
  0.0 92.7 jit_solution(1292829702490594717)
XLA Ops:
  0.0 0.7 shard_map.64
  0.7 8.4 %all_gather.6.both_ref = f32[32,768]{1,0:T(8,128)S(1)} all-gather(f32[16,768]{1,0:T(8,128)S(1)} %shard_map.64), channel_id=1, replica_groups=mesh['side'=8,'host'=4,'core'=2,'tp'=8] {'core'}, dimensions={0}, use_global_device_ids=true | all-gather | bytes 147456 | tf_op jit(solution)/shard_map/all_gather | solution.py:184
  9.1 0.0 copy-start.1
  9.1 0.0 copy-start.2
  9.1 0.4 shard_map.65
  9.5 24.8 %all_to_all.30.slots_ref = bf16[32,8,768]{2,1,0:T(8,128)(2,1)S(1)} all-to-all(bf16[32,8,768]{2,1,0:T(8,128)(2,1)S(1)} %get-tuple-element.22), channel_id=1, replica_groups=mesh['side'=8,'host'=4,'core'=2,'tp'=8] {'host','tp'}, dimensions={0} | all-to-all | bytes 786432 | tf_op jit(solution)/shard_map/all_to_all | solution.py:195
  34.3 0.0 copy-done.1
  34.3 0.0 copy-done.2
  34.3 1.6 %shard_map.66 = (bf16[8,256,256]{2,1,0:T(8,128)(2,1)S(1)}, bf16[8,128,256]{2,1,0:T(8,128)(2,1)S(1)}, bf16[256,128]{1,0:T(8,128)(2,1)S(1)}, s32[1]{0:T(128)}) custom-call(bf16[32,8,768]{2,1,0:T(8,128)(2,1)S(1)} %all_to_all.30.slots_ref, bf16[1,768,1024]{2,1,0:T(8,128)(2,1)S(1)} %copy-done.1, bf16[1,768,1024]{2,1,0:T(8,128)(2,1)S(1)} %copy-done.2, ...), custom_call_target="tpu_custom_call" | custom-call | tf_op jit(solution)/shard_map/pallas_call | solution.py:196
  36.6 0.0 copy-start
  36.6 20.3 %conditional.1 = (bf16[8,256,128]{2,1,0:T(8,128)(2,1)S(1)}) conditional(s32[]{:T(128)} %bitcast.3, bf16[8,256,256]{2,1,0:T(8,128)(2,1)S(1)} %get-tuple-element.24, (bf16[8,128,256]{2,1,0:T(8,128)(2,1)S(1)}, bf16[256,128]{1,0:T(8,128)(2,1)S(1)}) %tuple.11), branch_computations={%region_0.0_spmd, %region_1.0_spmd} | conditional | bytes 3145736 | solution.py:208
  36.6 11.4 %all_to_all.28.parts_ref = bf16[8,128,256]{2,1,0:T(8,128)(2,1)S(1)} all-to-all(bf16[8,128,256]{2,1,0:T(8,128)(2,1)S(1)} %get-tuple-element.14), channel_id=1, replica_groups=mesh['side'=8,'host'=4,'core'=2,'tp'=8] {'side'}, dimensions={0} | all-to-all | bytes 1048576 | tf_op jit(solution)/shard_map/cond/branch_1_fun/all_to_all | solution.py:149
  48.0 0.1 branch_1_fun.2
  48.1 8.5 %all_to_all.29.hidden_ref = bf16[8,128,128]{2,1,0:T(8,128)(2,1)S(1)} all-to-all(bf16[8,128,128]{2,1,0:T(8,128)(2,1)S(1)} %branch_1_fun.2), channel_id=1, replica_groups=mesh['side'=8,'host'=4,'core'=2,'tp'=8] {'side'}, dimensions={0} | all-to-all | bytes 524288 | tf_op jit(solution)/shard_map/cond/branch_1_fun/all_to_all | solution.py:157
  56.6 0.3 branch_1_fun.3
  56.9 0.0 copy-done
  56.9 0.6 shard_map.67
  57.5 31.5 %all_to_all.31.parts_ref = bf16[32,8,768]{2,1,0:T(8,128)(2,1)S(1)} all-to-all(bf16[32,8,768]{2,1,0:T(8,128)(2,1)S(1)} %shard_map.67), channel_id=1, replica_groups=mesh['side'=8,'host'=4,'core'=2,'tp'=8] {'host','tp'}, dimensions={0} | all-to-all | bytes 786432 | tf_op jit(solution)/shard_map/all_to_all | solution.py:216
  89.0 0.2 shard_map.68
  89.2 2.8 %all_gather.7.both_ref = f32[4,8,768]{2,1,0:T(8,128)S(1)} all-gather(f32[2,8,768]{2,1,0:T(8,128)S(1)} %shard_map.68), channel_id=1, replica_groups=mesh['side'=8,'host'=4,'core'=2,'tp'=8] {'core'}, dimensions={0}, use_global_device_ids=true | all-gather | bytes 147456 | tf_op jit(solution)/shard_map/all_gather | solution.py:224
  92.1 0.6 shard_map.69
Async XLA Ops:
  9.1 25.2 %copy-start.1 = (bf16[1,768,1024]{2,1,0:T(8,128)(2,1)S(1)}, bf16[1,768,1024]{2,1,0:T(8,128)(2,1)}, u32[]{:S(2)}) copy-start(bf16[1,768,1024]{2,1,0:T(8,128)(2,1)} %gate_ref.1) | copy-start | bytes 4718596
  9.1 25.2 %copy-start.2 = (bf16[1,768,1024]{2,1,0:T(8,128)(2,1)S(1)}, bf16[1,768,1024]{2,1,0:T(8,128)(2,1)}, u32[]{:S(2)}) copy-start(bf16[1,768,1024]{2,1,0:T(8,128)(2,1)} %up_ref.1) | copy-start | bytes 4718596
  36.6 20.3 %copy-start = (bf16[1,1024,768]{2,1,0:T(8,128)(2,1)S(1)}, bf16[1,1024,768]{2,1,0:T(8,128)(2,1)}, u32[]{:S(2)}) copy-start(bf16[1,1024,768]{2,1,0:T(8,128)(2,1)} %down_ref.1) | copy-start | bytes 4718596

commit v5 on v4

--- a/solution.py
+++ b/solution.py
@@ -92,24 +92,19 @@
     used = (slots[:, 0:1].astype(F32) < EMPTY / 2).astype(F32)
     count = jnp.sum(used).astype(jnp.int32)
     count_ref[0] = count
-
-    def parts(slots, ref_out):
-        for pair in range(SIDE // 2):
-            cols = slice(256 * pair, 256 * pair + 256)
-            for half, ref in enumerate((gate_ref, up_ref)):
-                part = jnp.dot(slots, ref[0, :, cols], preferred_element_type=F32).astype(BF)
-                ref_out[2 * pair, :, 128 * half : 128 * half + 128] = part[:, 0:128]
-                ref_out[2 * pair + 1, :, 128 * half : 128 * half + 128] = part[:, 128:256]
-
-    @pl.when(count > FEW)
-    def _():
-        parts(slots, out_ref)
+    for pair in range(SIDE // 2):
+        cols = slice(256 * pair, 256 * pair + 256)
+        for half, ref in enumerate((gate_ref, up_ref)):
+            part = jnp.dot(slots, ref[0, :, cols], preferred_element_type=F32).astype(BF)
+            out_ref[2 * pair, :, 128 * half : 128 * half + 128] = part[:, 0:128]
+            out_ref[2 * pair + 1, :, 128 * half : 128 * half + 128] = part[:, 128:256]
 
     @pl.when(count <= FEW)
     def _():
         front, spread = places(used)
         spread_ref[...] = spread
-        parts(jnp.dot(front, slots, preferred_element_type=F32).astype(BF), few_ref)
+        for s in range(SIDE):
+            few_ref[s] = jnp.dot(front, out_ref[s], preferred_element_type=F32).astype(BF)
 
 
 def hidden_kernel(parts_ref, out_ref):
@@ -124,7 +119,8 @@
 
 def back_kernel(spread_ref, hidden_ref, out_ref):
     for s in range(SIDE):
-        out_ref[s] = jnp.dot(spread_ref[...], hidden_ref[s], preferred_element_type=F32).astype(BF)
+        spread = spread_ref[:, 0 : hidden_ref.shape[1]]
+        out_ref[s] = jnp.dot(spread, hidden_ref[s], preferred_element_type=F32).astype(BF)
 
 
 def down_kernel(hidden_ref, down_ref, out_ref):
@@ -161,14 +157,14 @@
     return middle(parts)
 
 
-def few(parts, few_parts, spread):
+def few(rows, parts, few_parts, spread):
     return pl.pallas_call(
         back_kernel,
         out_shape=jax.ShapeDtypeStruct((SIDE, 256, 128), BF),
         in_specs=[VM, VM],
         out_specs=VM,
         compiler_params=LIMIT,
-    )(spread, middle(few_parts))
+    )(spread, middle(few_parts[:, :rows]))
 
 
 def local(rows, expert_ids, combine, w_gate, w_up, w_down):
@@ -205,7 +201,9 @@
         out_specs=(VM, VM, VM, SM),
         compiler_params=LIMIT,
     )(slots, near(w_gate), near(w_up), far(w_down))
-    hidden = lax.cond(count[0] <= FEW, few, many, parts, few_parts, spread)
+    size = (count[0] > FEW // 2).astype(jnp.int32) + (count[0] > FEW).astype(jnp.int32)
+    sizes = [functools.partial(few, FEW // 2), functools.partial(few, FEW), many]
+    hidden = lax.switch(size, sizes, parts, few_parts, spread)
     outs = pl.pallas_call(
         down_kernel,
         out_shape=jax.ShapeDtypeStruct((32, 8, width), BF),

time: 91.9 us -> 90.2 us (0.982); the launches traced: 92.7 us -> 89.9 us
  blocking collectives: 87.5 us -> 84.4 us
    all_to_all x1, blocking collectives: 31.5 us -> 18.9 us  [local(): outs = lax.all_to_all(outs, ('host', 'tp'), 0, 0, tiled=True)]
    all_to_all x1, blocking collectives: 11.4 us -> 15.6 us  [middle(): parts = lax.all_to_all(parts, 'side', 0, 0, tiled=True)]
    all_to_all x1, blocking collectives: 8.49 us -> 11.5 us  [middle(): return lax.all_to_all(hidden, 'side', 0, 0, tiled=True)]
    all_gather x1, blocking collectives: 2.83 us -> 5.14 us  [local(): mixed = lax.all_gather(mixed, 'core', axis=0, tiled=True)]
where the time goes in v5:
time: 90.2 us; the launch traced here: 89.9 us
  blocking collectives  84.4 us (94%)
  Pallas kernels  4.14 us (5%)
  between operations  1.33 us (1%)
    all_to_all x1, blocking collectives, local(): slots = lax.all_to_all(slots, ('host', 'tp'), 0, 0, tiled=True)  24.8 us
    all_to_all x1, blocking collectives, local(): outs = lax.all_to_all(outs, ('host', 'tp'), 0, 0, tiled=True)  18.9 us
    all_to_all x1, blocking collectives, middle(): parts = lax.all_to_all(parts, 'side', 0, 0, tiled=True)  15.6 us
    all_to_all x1, blocking collectives, middle(): return lax.all_to_all(hidden, 'side', 0, 0, tiled=True)  11.5 us
    all_gather x1, blocking collectives, local(): both = lax.all_gather(mine, 'core', axis=0, tiled=True)  8.39 us
    all_gather x1, blocking collectives, local(): mixed = lax.all_gather(mixed, 'core', axis=0, tiled=True)  5.14 us

profile of v5, /device:TPU:1, one launch (start us, length us, event | category | flops | bytes accessed | tf_op | source)
XLA Modules:
  0.0 89.9 jit_solution(4308433224550665046)
XLA Ops:
  0.0 0.7 shard_map.64
  0.7 8.4 %all_gather.6.both_ref = f32[32,768]{1,0:T(8,128)S(1)} all-gather(f32[16,768]{1,0:T(8,128)S(1)} %shard_map.64), channel_id=1, replica_groups=mesh['side'=8,'host'=4,'core'=2,'tp'=8] {'core'}, dimensions={0}, use_global_device_ids=true | all-gather | bytes 147456 | tf_op jit(solution)/shard_map/all_gather | solution.py:180
  9.1 0.0 copy-start.1
  9.1 0.0 copy-start.2
  9.1 0.4 shard_map.65
  9.5 24.8 %all_to_all.40.slots_ref = bf16[32,8,768]{2,1,0:T(8,128)(2,1)S(1)} all-to-all(bf16[32,8,768]{2,1,0:T(8,128)(2,1)S(1)} %get-tuple-element.29), channel_id=1, replica_groups=mesh['side'=8,'host'=4,'core'=2,'tp'=8] {'host','tp'}, dimensions={0} | all-to-all | bytes 786432 | tf_op jit(solution)/shard_map/all_to_all | solution.py:191
  34.3 0.0 copy-done.1
  34.3 0.0 copy-done.2
  34.3 1.5 %shard_map.66 = (bf16[8,256,256]{2,1,0:T(8,128)(2,1)S(1)}, bf16[8,128,256]{2,1,0:T(8,128)(2,1)S(1)}, bf16[256,128]{1,0:T(8,128)(2,1)S(1)}, s32[1]{0:T(128)}) custom-call(bf16[32,8,768]{2,1,0:T(8,128)(2,1)S(1)} %all_to_all.40.slots_ref, bf16[1,768,1024]{2,1,0:T(8,128)(2,1)S(1)} %copy-done.1, bf16[1,768,1024]{2,1,0:T(8,128)(2,1)S(1)} %copy-done.2, ...), custom_call_target="tpu_custom_call" | custom-call | tf_op jit(solution)/shard_map/pallas_call | solution.py:192
  37.1 0.0 copy-start
  37.1 27.3 %conditional.1 = (bf16[8,256,128]{2,1,0:T(8,128)(2,1)S(1)}) conditional(s32[]{:T(128)} %bitcast.3, (bf16[8,128,256]{2,1,0:T(8,128)(2,1)S(1)}, bf16[256,128]{1,0:T(8,128)(2,1)S(1)}) %tuple.14, (bf16[8,128,256]{2,1,0:T(8,128)(2,1)S(1)}, bf16[256,128]{1,0:T(8,128)(2,1)S(1)}) %tuple.14, ...), branch_computations={%region_0.0_spmd, %region_1.0_spmd, %region_2.0_spmd} | conditional | bytes 3145736 | solution.py:206
  37.2 15.6 %all_to_all.38.parts_ref = bf16[8,256,256]{2,1,0:T(8,128)(2,1)S(1)} all-to-all(bf16[8,256,256]{2,1,0:T(8,128)(2,1)S(1)} %param.2), channel_id=1, replica_groups=mesh['side'=8,'host'=4,'core'=2,'tp'=8] {'side'}, dimensions={0} | all-to-all | bytes 2097152 | tf_op jit(solution)/shard_map/cond/branch_2_fun/all_to_all | solution.py:145
  52.8 0.2 branch_2_fun.1
  52.9 11.5 %all_to_all.39 = bf16[8,256,128]{2,1,0:T(8,128)(2,1)S(1)} all-to-all(bf16[8,256,128]{2,1,0:T(8,128)(2,1)S(1)} %branch_2_fun.1), channel_id=1, replica_groups=mesh['side'=8,'host'=4,'core'=2,'tp'=8] {'side'}, dimensions={0} | all-to-all | bytes 1048576 | tf_op jit(solution)/shard_map/cond/branch_2_fun/all_to_all | solution.py:153
  64.5 0.0 copy-done
  64.5 0.6 shard_map.67
  65.1 18.9 %all_to_all.41.parts_ref = bf16[32,8,768]{2,1,0:T(8,128)(2,1)S(1)} all-to-all(bf16[32,8,768]{2,1,0:T(8,128)(2,1)S(1)} %shard_map.67), channel_id=1, replica_groups=mesh['side'=8,'host'=4,'core'=2,'tp'=8] {'host','tp'}, dimensions={0} | all-to-all | bytes 786432 | tf_op jit(solution)/shard_map/all_to_all | solution.py:214
  84.0 0.2 shard_map.68
  84.2 5.1 %all_gather.7.both_ref = f32[4,8,768]{2,1,0:T(8,128)S(1)} all-gather(f32[2,8,768]{2,1,0:T(8,128)S(1)} %shard_map.68), channel_id=1, replica_groups=mesh['side'=8,'host'=4,'core'=2,'tp'=8] {'core'}, dimensions={0}, use_global_device_ids=true | all-gather | bytes 147456 | tf_op jit(solution)/shard_map/all_gather | solution.py:222
  89.3 0.6 shard_map.69
Async XLA Ops:
  9.1 25.2 %copy-start.1 = (bf16[1,768,1024]{2,1,0:T(8,128)(2,1)S(1)}, bf16[1,768,1024]{2,1,0:T(8,128)(2,1)}, u32[]{:S(2)}) copy-start(bf16[1,768,1024]{2,1,0:T(8,128)(2,1)} %gate_ref.1) | copy-start | bytes 4718596
  9.1 25.2 %copy-start.2 = (bf16[1,768,1024]{2,1,0:T(8,128)(2,1)S(1)}, bf16[1,768,1024]{2,1,0:T(8,128)(2,1)}, u32[]{:S(2)}) copy-start(bf16[1,768,1024]{2,1,0:T(8,128)(2,1)} %up_ref.1) | copy-start | bytes 4718596
  37.1 27.3 %copy-start = (bf16[1,1024,768]{2,1,0:T(8,128)(2,1)S(1)}, bf16[1,1024,768]{2,1,0:T(8,128)(2,1)}, u32[]{:S(2)}) copy-start(bf16[1,1024,768]{2,1,0:T(8,128)(2,1)} %down_ref.1) | copy-start | bytes 4718596

commit v6 on v5

--- a/solution.py
+++ b/solution.py
@@ -119,8 +119,7 @@
 
 def back_kernel(spread_ref, hidden_ref, out_ref):
     for s in range(SIDE):
-        spread = spread_ref[:, 0 : hidden_ref.shape[1]]
-        out_ref[s] = jnp.dot(spread, hidden_ref[s], preferred_element_type=F32).astype(BF)
+        out_ref[s] = jnp.dot(spread_ref[...], hidden_ref[s], preferred_element_type=F32).astype(BF)
 
 
 def down_kernel(hidden_ref, down_ref, out_ref):
@@ -157,14 +156,14 @@
     return middle(parts)
 
 
-def few(rows, parts, few_parts, spread):
+def few(parts, few_parts, spread):
     return pl.pallas_call(
         back_kernel,
         out_shape=jax.ShapeDtypeStruct((SIDE, 256, 128), BF),
         in_specs=[VM, VM],
         out_specs=VM,
         compiler_params=LIMIT,
-    )(spread, middle(few_parts[:, :rows]))
+    )(spread, middle(few_parts))
 
 
 def local(rows, expert_ids, combine, w_gate, w_up, w_down):
@@ -201,9 +200,7 @@
         out_specs=(VM, VM, VM, SM),
         compiler_params=LIMIT,
     )(slots, near(w_gate), near(w_up), far(w_down))
-    size = (count[0] > FEW // 2).astype(jnp.int32) + (count[0] > FEW).astype(jnp.int32)
-    sizes = [functools.partial(few, FEW // 2), functools.partial(few, FEW), many]
-    hidden = lax.switch(size, sizes, parts, few_parts, spread)
+    hidden = lax.cond(count[0] <= FEW, few, many, parts, few_parts, spread)
     outs = pl.pallas_call(
         down_kernel,
         out_shape=jax.ShapeDtypeStruct((32, 8, width), BF),

time: 90.2 us -> 90.6 us (level)
    all_gather x1, blocking collectives: 5.14 us -> 9.44 us  [local(): mixed = lax.all_gather(mixed, 'core', axis=0, tiled=True)]
    all_to_all x1, blocking collectives: 15.6 us -> 11.4 us  [middle(): parts = lax.all_to_all(parts, 'side', 0, 0, tiled=True)]
    all_to_all x1, blocking collectives: 18.9 us -> 22.1 us  [local(): outs = lax.all_to_all(outs, ('host', 'tp'), 0, 0, tiled=True)]
    all_to_all x1, blocking collectives: 11.5 us -> 8.49 us  [middle(): return lax.all_to_all(hidden, 'side', 0, 0, tiled=True)]
where the time goes in v6:
time: 90.6 us; the launch traced here: 90.3 us
  blocking collectives  84.7 us (93%)
  Pallas kernels  4.86 us (5%)
    all_to_all x1, blocking collectives, local(): slots = lax.all_to_all(slots, ('host', 'tp'), 0, 0, tiled=True)  24.8 us
    all_to_all x1, blocking collectives, local(): outs = lax.all_to_all(outs, ('host', 'tp'), 0, 0, tiled=True)  22.1 us
    all_to_all x1, blocking collectives, middle(): parts = lax.all_to_all(parts, 'side', 0, 0, tiled=True)  11.4 us
    all_gather x1, blocking collectives, local(): mixed = lax.all_gather(mixed, 'core', axis=0, tiled=True)  9.44 us
    all_to_all x1, blocking collectives, middle(): return lax.all_to_all(hidden, 'side', 0, 0, tiled=True)  8.49 us
    all_gather x1, blocking collectives, local(): both = lax.all_gather(mine, 'core', axis=0, tiled=True)  8.39 us
    pallas_call x1, Pallas kernels, local(): pl.pallas_call(up_kernel, out_shape=(jax.ShapeDtypeStruct((SIDE, 256, 256...  2.03 us

profile of v6, /device:TPU:1, one launch (start us, length us, event | category | flops | bytes accessed | tf_op | source)
XLA Modules:
  0.0 90.3 jit_solution(9982165350452205404)
XLA Ops:
  0.0 0.7 shard_map.64
  0.7 8.4 %all_gather.6.both_ref = f32[32,768]{1,0:T(8,128)S(1)} all-gather(f32[16,768]{1,0:T(8,128)S(1)} %shard_map.64), channel_id=1, replica_groups=mesh['side'=8,'host'=4,'core'=2,'tp'=8] {'core'}, dimensions={0}, use_global_device_ids=true | all-gather | bytes 147456 | tf_op jit(solution)/shard_map/all_gather | solution.py:179
  9.1 0.0 copy-start.1
  9.1 0.0 copy-start.2
  9.1 0.4 shard_map.65
  9.5 24.8 %all_to_all.30.slots_ref = bf16[32,8,768]{2,1,0:T(8,128)(2,1)S(1)} all-to-all(bf16[32,8,768]{2,1,0:T(8,128)(2,1)S(1)} %get-tuple-element.22), channel_id=1, replica_groups=mesh['side'=8,'host'=4,'core'=2,'tp'=8] {'host','tp'}, dimensions={0} | all-to-all | bytes 786432 | tf_op jit(solution)/shard_map/all_to_all | solution.py:190
  34.3 0.0 copy-done.1
  34.3 0.0 copy-done.2
  34.3 2.0 %shard_map.66 = (bf16[8,256,256]{2,1,0:T(8,128)(2,1)S(1)}, bf16[8,128,256]{2,1,0:T(8,128)(2,1)S(1)}, bf16[256,128]{1,0:T(8,128)(2,1)S(1)}, s32[1]{0:T(128)}) custom-call(bf16[32,8,768]{2,1,0:T(8,128)(2,1)S(1)} %all_to_all.30.slots_ref, bf16[1,768,1024]{2,1,0:T(8,128)(2,1)S(1)} %copy-done.1, bf16[1,768,1024]{2,1,0:T(8,128)(2,1)S(1)} %copy-done.2, ...), custom_call_target="tpu_custom_call" | custom-call | tf_op jit(solution)/shard_map/pallas_call | solution.py:191
  37.0 0.0 copy-start
  37.0 20.3 %conditional.1 = (bf16[8,256,128]{2,1,0:T(8,128)(2,1)S(1)}) conditional(s32[]{:T(128)} %bitcast.3, bf16[8,256,256]{2,1,0:T(8,128)(2,1)S(1)} %get-tuple-element.24, (bf16[8,128,256]{2,1,0:T(8,128)(2,1)S(1)}, bf16[256,128]{1,0:T(8,128)(2,1)S(1)}) %tuple.11), branch_computations={%region_0.0_spmd, %region_1.0_spmd} | conditional | bytes 3145736 | solution.py:203
  37.0 11.4 %all_to_all.28.parts_ref = bf16[8,128,256]{2,1,0:T(8,128)(2,1)S(1)} all-to-all(bf16[8,128,256]{2,1,0:T(8,128)(2,1)S(1)} %get-tuple-element.14), channel_id=1, replica_groups=mesh['side'=8,'host'=4,'core'=2,'tp'=8] {'side'}, dimensions={0} | all-to-all | bytes 1048576 | tf_op jit(solution)/shard_map/cond/branch_1_fun/all_to_all | solution.py:144
  48.5 0.1 branch_1_fun.2
  48.6 8.5 %all_to_all.29.hidden_ref = bf16[8,128,128]{2,1,0:T(8,128)(2,1)S(1)} all-to-all(bf16[8,128,128]{2,1,0:T(8,128)(2,1)S(1)} %branch_1_fun.2), channel_id=1, replica_groups=mesh['side'=8,'host'=4,'core'=2,'tp'=8] {'side'}, dimensions={0} | all-to-all | bytes 524288 | tf_op jit(solution)/shard_map/cond/branch_1_fun/all_to_all | solution.py:152
  57.0 0.3 branch_1_fun.3
  57.3 0.0 copy-done
  57.3 0.6 shard_map.67
  57.9 22.1 %all_to_all.31.parts_ref = bf16[32,8,768]{2,1,0:T(8,128)(2,1)S(1)} all-to-all(bf16[32,8,768]{2,1,0:T(8,128)(2,1)S(1)} %shard_map.67), channel_id=1, replica_groups=mesh['side'=8,'host'=4,'core'=2,'tp'=8] {'host','tp'}, dimensions={0} | all-to-all | bytes 786432 | tf_op jit(solution)/shard_map/all_to_all | solution.py:211
  80.0 0.2 shard_map.68
  80.2 9.4 %all_gather.7.both_ref = f32[4,8,768]{2,1,0:T(8,128)S(1)} all-gather(f32[2,8,768]{2,1,0:T(8,128)S(1)} %shard_map.68), channel_id=1, replica_groups=mesh['side'=8,'host'=4,'core'=2,'tp'=8] {'core'}, dimensions={0}, use_global_device_ids=true | all-gather | bytes 147456 | tf_op jit(solution)/shard_map/all_gather | solution.py:219
  89.7 0.6 shard_map.69
Async XLA Ops:
  9.1 25.2 %copy-start.1 = (bf16[1,768,1024]{2,1,0:T(8,128)(2,1)S(1)}, bf16[1,768,1024]{2,1,0:T(8,128)(2,1)}, u32[]{:S(2)}) copy-start(bf16[1,768,1024]{2,1,0:T(8,128)(2,1)} %gate_ref.1) | copy-start | bytes 4718596
  9.1 25.2 %copy-start.2 = (bf16[1,768,1024]{2,1,0:T(8,128)(2,1)S(1)}, bf16[1,768,1024]{2,1,0:T(8,128)(2,1)}, u32[]{:S(2)}) copy-start(bf16[1,768,1024]{2,1,0:T(8,128)(2,1)} %up_ref.1) | copy-start | bytes 4718596
  37.0 20.3 %copy-start = (bf16[1,1024,768]{2,1,0:T(8,128)(2,1)S(1)}, bf16[1,1024,768]{2,1,0:T(8,128)(2,1)}, u32[]{:S(2)}) copy-start(bf16[1,1024,768]{2,1,0:T(8,128)(2,1)} %down_ref.1) | copy-start | bytes 4718596
